TPU v7x, 256 devices: a whole 4x4x8 slice. The times are simulated.
256 devices in a mesh: blk: 32 (over x, z), grp: 8 (over y, core).
Axes of the slice: x: 4, y: 4, z: 8, core: 2. Of those that a mesh axis runs over, the one named last changes fastest.
Arguments:
- features: bfloat16 [8, 8192, 256], P('grp', 'blk'), may hold values from -6 to 6
- weight: bfloat16 [256, 256], replicated, may hold values from -0.375 to 0.375
- cotangent: bfloat16 [8, 8192, 256], P('grp', 'blk'), may hold values from -6 to 6
- dense_tiles: bfloat16 [8, 32, 64, 128, 128], P('grp', 'blk'), as said below
- dense_cols: int32 [8, 32, 64], P('grp', 'blk'), may hold values from 0 to 1, as said below
- sparse_tiles: bfloat16 [8, 32, 32, 128, 128], P('grp', 'blk'), may hold values from -0.09375 to 0.09375
- sparse_rows: int32 [8, 32, 32], P('grp', 'blk'), may hold values from 0 to 1
- sparse_cols: int32 [8, 32, 32], P('grp', 'blk'), may hold values from 0 to 7
- send_rows: int32 [8, 32, 8, 128], P('grp', 'blk'), may hold values from 0 to 255
- send_counts: int32 [8, 32, 8], P('grp', 'blk'), may hold values from 16 to 128, as said below
Outputs:
- hidden: bfloat16 [8, 8192, 256], P('grp', 'blk')
- grad_features: bfloat16 [8, 8192, 256], P('grp', 'blk')
- grad_weight: float32 [256, 256], replicated
Inputs may be any that keep to these rules, and one draw needn't show every extreme that they name: Tile t of device (g, b) has row tile t % 2 and source block t // 2; for one device and one source block the 2 tiles name distinct column tiles, and the adjacency given by dense_tiles and dense_cols inside each group is symmetric. `dense_tiles`: together with dense_cols the tiles give a symmetric adjacency inside each group. `send_counts`: entry [s, b, g] counts the rows that device (s, b) sends to device (g, b); for every block index some receiver gets 128 rows from every sender.
All inputs are finite; a program needn't handle non-finite values.
Results may differ from a plain program's by a relative error of at most 0.0065.
Values may be sent and summed in bfloat16 or wider, within the bound.
No kernel may reach another device: no remote copies, remote signals or barrier semaphores. Data moves between devices by JAX's collectives and lax.ppermute only.
A program may use at most 64 MiB of HBM per device.

v0:
```python
import jax
import jax.numpy as jnp
from jax import lax
from jax.sharding import PartitionSpec as P


def body(
    features,
    weight,
    cotangent,
    dense_tiles,
    dense_cols,
    sparse_tiles,
    sparse_rows,
    sparse_cols,
    send_rows,
    send_counts,
):
    row_count = features.shape[1]
    hidden_width = weight.shape[1]
    tile_values = dense_tiles[0, 0]
    tile_cols = dense_cols[0, 0]
    tile_size = tile_values.shape[-1]
    row_tiles = row_count // tile_size
    projected = jnp.dot(features[0], weight, preferred_element_type=jnp.float32).astype(
        jnp.bfloat16
    )
    send_list = send_rows[0, 0]
    send_count = send_counts[0, 0]
    capacity = send_list.shape[1]
    in_use = jnp.arange(capacity)[None, :] < send_count[:, None]
    outgoing = jnp.where(in_use[:, :, None], projected[send_list], jnp.zeros((), jnp.bfloat16))
    received = lax.all_to_all(outgoing, "grp", split_axis=0, concat_axis=0, tiled=True)
    shards = lax.all_gather(projected, "blk", axis=0, tiled=True)
    block_count = shards.shape[0] // row_count
    chosen = tile_values
    chosen_cols = tile_cols
    positions = jnp.arange(block_count * row_tiles) // row_tiles * row_tiles + chosen_cols
    source = shards.reshape(block_count * row_tiles, tile_size, hidden_width)[positions]
    dense_part = jnp.einsum(
        "crij,crjh->rih",
        chosen.reshape(block_count, row_tiles, tile_size, tile_size),
        source.reshape(block_count, row_tiles, tile_size, hidden_width),
        preferred_element_type=jnp.float32,
    )
    sparse_vals = sparse_tiles[0, 0]
    row_slot = sparse_rows[0, 0]
    col_block = sparse_cols[0, 0]
    recv_count = received.shape[0]
    products = jnp.einsum(
        "uij,ujh->uih", sparse_vals, received[col_block], preferred_element_type=jnp.float32
    )
    row_pick = (row_slot[:, None] == jnp.arange(row_tiles)[None, :]).astype(jnp.float32)
    sparse_part = jnp.einsum("ur,uih->rih", row_pick, products, precision=lax.Precision.HIGHEST)
    pre_act = (dense_part + sparse_part).reshape(row_count, hidden_width)
    sigmoid_pre = jax.nn.sigmoid(pre_act)
    hidden = (pre_act * sigmoid_pre).astype(jnp.bfloat16)
    grad_pre = (
        cotangent[0].astype(jnp.float32) * sigmoid_pre * (1.0 + pre_act * (1.0 - sigmoid_pre))
    ).astype(jnp.bfloat16)
    grad_tiles = grad_pre.reshape(row_tiles, tile_size, hidden_width)
    block_count = row_count * lax.axis_size("blk") // row_count
    chosen = tile_values
    chosen_cols = tile_cols
    chosen = chosen.reshape(block_count, row_tiles, tile_size, tile_size)
    chosen_cols = chosen_cols.reshape(block_count, row_tiles)
    moved = jnp.einsum("crij,rih->crjh", chosen, grad_tiles, preferred_element_type=jnp.float32)
    pieces = [
        jnp.sum(jnp.where((chosen_cols == target)[:, :, None, None], moved, 0.0), axis=1)
        for target in range(row_tiles)
    ]
    dense_back = lax.psum_scatter(
        jnp.stack(pieces, axis=1).reshape(row_count * lax.axis_size("blk"), hidden_width),
        "blk",
        scatter_dimension=0,
        tiled=True,
    )
    tile_grads = jnp.einsum(
        "uij,uih->ujh", sparse_vals, grad_tiles[row_slot], preferred_element_type=jnp.float32
    )
    block_pick = (col_block[:, None] == jnp.arange(recv_count)[None, :]).astype(jnp.float32)
    slot_grad = jnp.einsum("uq,ujh->qjh", block_pick, tile_grads, precision=lax.Precision.HIGHEST)
    returned = lax.all_to_all(slot_grad, "grp", split_axis=0, concat_axis=0, tiled=True)
    returned = jnp.where(in_use[:, :, None], returned, 0.0)
    sparse_back = (
        jnp.zeros((row_count, hidden_width), jnp.float32)
        .at[send_list.reshape(-1)]
        .add(returned.reshape(-1, hidden_width))
    )
    agg_grad = (dense_back + sparse_back).astype(jnp.bfloat16)
    grad_features = jnp.einsum(
        "rh,fh->rf", agg_grad, weight, preferred_element_type=jnp.float32
    ).astype(jnp.bfloat16)
    partial_weight = jnp.einsum(
        "rf,rh->fh", features[0], agg_grad, preferred_element_type=jnp.float32
    )
    vertex_total = row_count * lax.axis_size("blk") * lax.axis_size("grp")
    grad_weight = lax.psum(partial_weight, ("blk", "grp")) * float(vertex_total) ** (-0.5)
    return (hidden[None], grad_features[None], grad_weight)


def solution(mesh):
    placed = (
        P("grp", "blk", None),
        P(),
        P("grp", "blk", None),
        P("grp", "blk", None, None, None),
        P("grp", "blk", None),
        P("grp", "blk", None, None, None),
        P("grp", "blk", None),
        P("grp", "blk", None),
        P("grp", "blk", None, None),
        P("grp", "blk", None),
    )
    return jax.shard_map(
        body,
        mesh=mesh,
        in_specs=placed,
        out_specs=(P("grp", "blk", None), P("grp", "blk", None), P()),
        check_vma=False,
    )
```

profile of v0, /device:TPU:2, one launch (start us, length us, event | category | flops | bytes accessed | tf_op | source)
XLA Modules:
  0.0 613.4 jit_solution(7899231333244268528)
XLA Ops:
  7.3 1.9 convolution_convert_fusion.1
  9.2 0.7 fusion.20
  9.9 4.4 gather_fusion.1
  14.4 1.0 broadcast_select_fusion.1
  15.4 4.5 all-to-all-start
  20.5 9.8 %all-to-all-done = bf16[8,128,256]{2,1,0:T(8,128)(2,1)S(1)} async-done(((bf16[8,128,256]{2,1,0:T(8,128)(2,1)}), bf16[8,128,256]{2,1,0:T(8,128)(2,1)S(1)}, u32[]{:S(2)}, u32[]{:S(2)}) %all-to-all-start) | async-done | bytes 524320 | tf_op jit(solution)/shard_map/all_to_all | solution.py:33
  30.2 2.0 gather_fusion.2
  32.3 4.6 convolution_bitcast_fusion.1
  36.9 5.5 copy.32
  42.4 3.6 fusion.25
  46.0 48.7 %all-gather.2.cloned.1.call-done = bf16[8192,256]{1,0:T(8,128)(2,1)} async-done(((bf16[256,256]{1,0:T(8,128)(2,1)}), bf16[8192,256]{1,0:T(8,128)(2,1)}) %all-gather.2.cloned.1.call-update) | async-done | bytes 4194320 | tf_op jit(solution)/shard_map/all_gather | solution.py:34
  94.7 5.0 gather_fusion
  99.7 3.0 fusion.9
  102.7 3.4 fusion
  106.0 3.8 pad_maximum_fusion
  109.8 9.0 %copy.38 = f32[32,2,128,256]{3,2,1,0:T(8,128)} copy(f32[32,2,128,256]{2,3,0,1:T(8,128)} %pad_maximum_fusion) | data formatting | bytes 16777216 | tf_op jit(solution)/shard_map/stack | solution.py:73
  118.8 2.0 gather_fusion.3
  120.9 4.3 convolution_bitcast_fusion
  125.1 5.5 copy.40
  130.6 3.7 fusion.22
  134.3 1.3 copy.41
  135.6 4.3 all-to-all-start.1
  140.1 15.8 %all-to-all-done.1 = f32[8,128,256]{2,1,0:T(8,128)} async-done(((f32[8,128,256]{2,1,0:T(8,128)}), f32[8,128,256]{2,1,0:T(8,128)}, u32[]{:S(2)}, u32[]{:S(2)}) %all-to-all-start.1) | async-done | bytes 1048608 | tf_op jit(solution)/shard_map/all_to_all | solution.py:83
  155.9 1.4 broadcast_select_fusion
  157.4 188.5 %reduce-scatter.2.cloned.1.call-done = f32[256,256]{1,0:T(8,128)} async-done(((f32[8192,256]{1,0:T(8,128)}), f32[256,256]{1,0:T(8,128)}) %reduce-scatter.2.cloned.1.call-update) | async-done | bytes 262160 | tf_op jit(solution)/shard_map/reduce_scatter | solution.py:72
  345.9 7.7 %scatter_fusion = f32[256,256]{1,0:T(8,128)} fusion(f32[256,256]{1,0:T(8,128)} %reduce-scatter.2.cloned.1.call-done, s32[1024]{0:T(1024)S(1)} %bitcast.110, f32[1024,256]{1,0:T(8,128)S(1)} %bitcast.103), kind=kCustom, calls=%fused_computation.4 | custom fusion | flops 262144 | bytes 3149824 | tf_op jit(solution)/shard_map/scatter-add | solution.py:88
  353.5 1.9 convolution_bitcast_fusion.3
  355.4 0.7 fusion.13
  356.2 1.9 fusion.5
  358.0 247.0 %all-reduce.2.cloned.1.call-done = f32[256,256]{0,1:T(8,128)} async-done(((f32[256,256]{0,1:T(8,128)}), f32[256,256]{0,1:T(8,128)}) %all-reduce.2.cloned.1.call-update) | async-done | bytes 262160 | tf_op jit(solution)/shard_map/psum | solution.py:98
  605.1 1.0 broadcast_multiply_fusion
  606.0 0.8 copy.42
  (37 shorter events, 0.9 us)
Async XLA Ops:
  7.2 92.5 %copy-start = (bf16[1,1,64,128,128]{4,3,2,1,0:T(8,128)(2,1)S(1)}, bf16[1,1,64,128,128]{4,3,2,1,0:T(8,128)(2,1)}, u32[]{:S(2)}) copy-start(bf16[1,1,64,128,128]{4,3,2,1,0:T(8,128)(2,1)} %param.13) | copy-start | bytes 6291460
  7.2 7.1 %copy-start.7 = (s32[1,1,8]{2,1,0:T(1,128)S(1)}, s32[1,1,8]{2,1,0:T(1,128)}, u32[]{:S(2)}) copy-start(s32[1,1,8]{2,1,0:T(1,128)} %param.19) | copy-start | bytes 100
  7.2 12.7 %copy-start.6 = (s32[1,1,32]{2,1,0:T(1,128)S(1)}, s32[1,1,32]{2,1,0:T(1,128)}, u32[]{:S(2)}) copy-start(s32[1,1,32]{2,1,0:T(1,128)} %param.17) | copy-start | bytes 388
  7.2 12.8 %copy-start.8 = (s32[1,1,64]{2,1,0:T(1,128)S(1)}, s32[1,1,64]{2,1,0:T(1,128)}, u32[]{:S(2)}) copy-start(s32[1,1,64]{2,1,0:T(1,128)} %param.14) | copy-start | bytes 772
  7.2 87.5 %all-gather.2.cloned.1.call-start = ((), (), s32[]{:S(2)}) async-start(), calls=%async_computation.3 | async-start | bytes 4325376 | tf_op jit(solution)/shard_map/all_gather | solution.py:34
  15.4 14.8 %all-to-all-start = ((bf16[8,128,256]{2,1,0:T(8,128)(2,1)}), bf16[8,128,256]{2,1,0:T(8,128)(2,1)S(1)}, u32[]{:S(2)}, u32[]{:S(2)}) async-start(bf16[8,128,256]{2,1,0:T(8,128)(2,1)} %broadcast_select_fusion.1), calls=%async_computation | async-start | bytes 1048576 | tf_op jit(solution)/shard_map/all_to_all | solution.py:33
  19.9 326.0 %reduce-scatter.2.cloned.1.call-start = ((), (), s32[]{:S(2)}) async-start(), calls=%async_computation.4 | async-start | bytes 8650752 | tf_op jit(solution)/shard_map/reduce_scatter | solution.py:72
  36.9 5.5 copy-start.5
  94.7 5.0 copy-start.3
  118.8 2.1 copy-start.1
  130.6 9.5 %copy-start.4 = (s32[1,1,8,128]{3,2,1,0:T(8,128)S(1)}, s32[1,1,8,128]{3,2,1,0:T(8,128)}, u32[]{:S(2)}) copy-start(s32[1,1,8,128]{3,2,1,0:T(8,128)} %param.18) | copy-start | bytes 12292
  135.6 20.4 %all-to-all-start.1 = ((f32[8,128,256]{2,1,0:T(8,128)}), f32[8,128,256]{2,1,0:T(8,128)}, u32[]{:S(2)}, u32[]{:S(2)}) async-start(f32[8,128,256]{2,1,0:T(8,128)} %copy.41), calls=%async_computation.2 | async-start | bytes 2097152 | tf_op jit(solution)/shard_map/all_to_all | solution.py:83
  139.9 465.2 %all-reduce.2.cloned.1.call-start = ((), (), s32[]{:S(2)}) async-start(), calls=%async_computation.5 | async-start | bytes 524288 | tf_op jit(solution)/shard_map/psum | solution.py:98
  345.9 7.7 %copy-start.2 = (bf16[1,256,256]{2,1,0:T(8,128)(2,1)S(1)}, bf16[1,256,256]{2,1,0:T(8,128)(2,1)}, u32[]{:S(2)}) copy-start(bf16[1,256,256]{2,1,0:T(8,128)(2,1)} %param.10) | copy-start | bytes 393220
Sparse Core Ops, SparseCore 0:
  11.2 83.4 all-gather.1
  118.9 226.8 reduce-scatter.1
  355.6 249.4 all-reduce.1
where the time goes:
time: 614 us; the launch traced here: 613 us
  waiting for transfers between devices  510 us (83%)
  local copies, waits for them, and re-layouts  36 us (6%)
  matrix products  28.2 us (5%)
  other arithmetic  16.4 us (3%)
  between operations  13.9 us (2%)
  starting transfers between devices  9.05 us (1%)
    psum x1, waiting for transfers between devices, body(): lax.psum(partial_weight, ('blk', 'grp')) * float(vertex_total) ** (-0.5)  247 us
    reduce_scatter x1, waiting for transfers between devices, body(): lax.psum_scatter(jnp.stack(pieces, axis=1).reshape(row_count * lax.axis_s...  188 us
    all_gather x1, waiting for transfers between devices, body(): shards = lax.all_gather(projected, 'blk', axis=0, tiled=True)  48.7 us
    all_to_all x1, waiting for transfers between devices, body(): lax.all_to_all(slot_grad, 'grp', split_axis=0, concat_axis=0, tiled=True)  15.8 us
  transfers between devices with their start and end apart: 5, of which 5 were waited for; matrix products, arithmetic and copies ran while one was open for 7% of the time, Pallas kernels for 0%

commit v1 on v0

--- a/solution.py
+++ b/solution.py
@@ -31,7 +31,9 @@
     in_use = jnp.arange(capacity)[None, :] < send_count[:, None]
     outgoing = jnp.where(in_use[:, :, None], projected[send_list], jnp.zeros((), jnp.bfloat16))
     received = lax.all_to_all(outgoing, "grp", split_axis=0, concat_axis=0, tiled=True)
-    shards = lax.all_gather(projected, "blk", axis=0, tiled=True)
+    shards = jnp.concatenate(
+        lax.all_to_all(jnp.stack([projected] * lax.axis_size("blk")), "blk", 0, 0), axis=0
+    )
     block_count = shards.shape[0] // row_count
     chosen = tile_values
     chosen_cols = tile_cols

time: 614 us -> 656 us (1.068)
  waiting for transfers between devices: 510 us -> 532 us
  blocking collectives: 0 us -> 14.7 us
    all_to_all x1, waiting for transfers between devices: 9.77 us -> 77.5 us  [body(): lax.all_to_all(jnp.stack([projected] * lax.axis_size('blk')), 'blk', 0, 0)]
    all_gather x1 -> x0, waiting for transfers between devices: 48.7 us -> none  [body(): shards = lax.all_gather(projected, 'blk', axis=0, tiled=True)]
    all_to_all x0 -> x1, blocking collectives: none -> 14.7 us  [body(): lax.all_to_all(outgoing, 'grp', split_axis=0, concat_axis=0, tiled=True)]
    all_to_all x1, starting transfers between devices: 4.47 us -> 11.8 us  [body(): lax.all_to_all(jnp.stack([projected] * lax.axis_size('blk')), 'blk', 0, 0)]
  transfers between devices with their start and end apart: 5 -> 4, of which waited for: 5 -> 4; matrix products, arithmetic and copies ran while one was open for 7% -> 5% of each run, Pallas kernels for 0% -> 0%
where the time goes in v1:
time: 656 us; the launch traced here: 655 us
  waiting for transfers between devices  532 us (81%)
  local copies, waits for them, and re-layouts  37.2 us (6%)
  matrix products  25.8 us (4%)
  starting transfers between devices  15.6 us (2%)
  other arithmetic  15.3 us (2%)
  blocking collectives  14.7 us (2%)
  between operations  14.2 us (2%)
    psum x1, waiting for transfers between devices, body(): lax.psum(partial_weight, ('blk', 'grp')) * float(vertex_total) ** (-0.5)  247 us
    reduce_scatter x1, waiting for transfers between devices, body(): lax.psum_scatter(jnp.stack(pieces, axis=1).reshape(row_count * lax.axis_s...  192 us
    all_to_all x1, waiting for transfers between devices, body(): lax.all_to_all(jnp.stack([projected] * lax.axis_size('blk')), 'blk', 0, 0)  77.5 us
    all_to_all x1, waiting for transfers between devices, body(): lax.all_to_all(slot_grad, 'grp', split_axis=0, concat_axis=0, tiled=True)  15.6 us
    all_to_all x1, blocking collectives, body(): lax.all_to_all(outgoing, 'grp', split_axis=0, concat_axis=0, tiled=True)  14.7 us
  transfers between devices with their start and end apart: 4, of which 4 were waited for; matrix products, arithmetic and copies ran while one was open for 5% of the time, Pallas kernels for 0%

profile of v1, /device:TPU:2, one launch (start us, length us, event | category | flops | bytes accessed | tf_op | source)
XLA Modules:
  0.0 654.7 jit_solution(16644800279967994650)
XLA Ops:
  7.2 0.8 fusion.20
  8.0 0.7 iota_compare_fusion.1
  8.8 1.2 convolution_convert_fusion.1
  9.9 3.9 gather_fusion.1
  14.1 14.7 %all_to_all.15 = bf16[8,128,256]{2,1,0:T(8,128)(2,1)S(1)} all-to-all(bf16[8,128,256]{2,1,0:T(8,128)(2,1)S(1)} %broadcast_select_fusion.1), channel_id=1, replica_groups=mesh['blk'=32,'grp'=8] {'grp'}, dimensions={0} | all-to-all | bytes 1048576 | tf_op jit(solution)/shard_map/all_to_all | solution.py:33
  28.7 2.4 stack.8
  31.2 11.8 %all-to-all-start = ((bf16[32,256,256]{2,1,0:T(8,128)(2,1)}), bf16[32,256,256]{2,1,0:T(8,128)(2,1)}, u32[]{:S(2)}, u32[]{:S(2)}) async-start(bf16[32,256,256]{2,1,0:T(8,128)(2,1)} %stack.8), calls=%async_computation | async-start | bytes 8388608 | tf_op jit(solution)/shard_map/all_to_all | solution.py:35
  43.5 2.0 gather_fusion.2
  45.6 4.6 convolution_bitcast_fusion.1
  50.1 5.5 copy.32
  55.7 3.6 fusion.25
  59.3 77.5 %all-to-all-done = bf16[32,256,256]{2,1,0:T(8,128)(2,1)} async-done(((bf16[32,256,256]{2,1,0:T(8,128)(2,1)}), bf16[32,256,256]{2,1,0:T(8,128)(2,1)}, u32[]{:S(2)}, u32[]{:S(2)}) %all-to-all-start) | async-done | bytes 4194336 | tf_op jit(solution)/shard_map/all_to_all | solution.py:35
  136.7 5.0 gather_fusion
  141.7 3.0 fusion.9
  144.7 3.4 fusion
  148.1 3.8 pad_maximum_fusion
  151.8 9.0 %copy.38 = f32[32,2,128,256]{3,2,1,0:T(8,128)} copy(f32[32,2,128,256]{2,3,0,1:T(8,128)} %pad_maximum_fusion) | data formatting | bytes 16777216 | tf_op jit(solution)/shard_map/stack | solution.py:75
  160.9 0.7 gather_fusion.3
  162.1 2.7 convolution_bitcast_fusion
  164.8 5.5 copy.40
  170.3 3.7 fusion.22
  173.9 1.4 copy.41
  175.3 3.6 all-to-all-start.2
  179.1 15.6 %all-to-all-done.2 = f32[8,128,256]{2,1,0:T(8,128)S(1)} async-done(((f32[8,128,256]{2,1,0:T(8,128)}), f32[8,128,256]{2,1,0:T(8,128)S(1)}, u32[]{:S(2)}, u32[]{:S(2)}) %all-to-all-start.2) | async-done | bytes 1048608 | tf_op jit(solution)/shard_map/all_to_all | solution.py:85
  195.0 191.8 %reduce-scatter.2.cloned.1.call-done = f32[256,256]{1,0:T(8,128)} async-done(((f32[8192,256]{1,0:T(8,128)}), f32[256,256]{1,0:T(8,128)}) %reduce-scatter.2.cloned.1.call-update) | async-done | bytes 262160 | tf_op jit(solution)/shard_map/reduce_scatter | solution.py:74
  386.7 7.8 %scatter_fusion = f32[256,256]{1,0:T(8,128)} fusion(f32[256,256]{1,0:T(8,128)} %reduce-scatter.2.cloned.1.call-done, s32[1024]{0:T(1024)S(1)} %bitcast.109, f32[1024,256]{1,0:T(8,128)S(1)} %bitcast.103), kind=kCustom, calls=%fused_computation.4 | custom fusion | flops 262144 | bytes 3149824 | tf_op jit(solution)/shard_map/scatter-add | solution.py:90
  394.5 1.9 convolution_bitcast_fusion.3
  396.4 0.7 fusion.13
  397.2 1.9 fusion.5
  399.0 247.0 %all-reduce.2.cloned.1.call-done = f32[256,256]{0,1:T(8,128)} async-done(((f32[256,256]{0,1:T(8,128)}), f32[256,256]{0,1:T(8,128)}) %all-reduce.2.cloned.1.call-update) | async-done | bytes 262160 | tf_op jit(solution)/shard_map/psum | solution.py:100
  646.0 1.0 broadcast_multiply_fusion
  647.0 0.8 copy.42
  (36 shorter events, 1.7 us)
Async XLA Ops:
  7.2 134.6 %copy-start = (bf16[1,1,64,128,128]{4,3,2,1,0:T(8,128)(2,1)S(1)}, bf16[1,1,64,128,128]{4,3,2,1,0:T(8,128)(2,1)}, u32[]{:S(2)}) copy-start(bf16[1,1,64,128,128]{4,3,2,1,0:T(8,128)(2,1)} %param.13) | copy-start | bytes 6291460
  31.2 11.9 %copy-start.8 = (s32[1,1,64]{2,1,0:T(1,128)S(1)}, s32[1,1,64]{2,1,0:T(1,128)}, u32[]{:S(2)}) copy-start(s32[1,1,64]{2,1,0:T(1,128)} %param.14) | copy-start | bytes 772
  31.2 12.3 %copy-start.7 = (s32[1,1,32]{2,1,0:T(1,128)S(1)}, s32[1,1,32]{2,1,0:T(1,128)}, u32[]{:S(2)}) copy-start(s32[1,1,32]{2,1,0:T(1,128)} %param.17) | copy-start | bytes 388
  31.2 105.5 %all-to-all-start = ((bf16[32,256,256]{2,1,0:T(8,128)(2,1)}), bf16[32,256,256]{2,1,0:T(8,128)(2,1)}, u32[]{:S(2)}, u32[]{:S(2)}) async-start(bf16[32,256,256]{2,1,0:T(8,128)(2,1)} %stack.8), calls=%async_computation | async-start | bytes 8388608 | tf_op jit(solution)/shard_map/all_to_all | solution.py:35
  43.0 343.7 %reduce-scatter.2.cloned.1.call-start = ((), (), s32[]{:S(2)}) async-start(), calls=%async_computation.4 | async-start | bytes 8650752 | tf_op jit(solution)/shard_map/reduce_scatter | solution.py:74
  50.1 5.5 copy-start.6
  136.7 5.0 copy-start.4
  160.8 1.2 copy-start.2
  170.3 8.8 %copy-start.5 = (s32[1,1,8,128]{3,2,1,0:T(8,128)S(1)}, s32[1,1,8,128]{3,2,1,0:T(8,128)}, u32[]{:S(2)}) copy-start(s32[1,1,8,128]{3,2,1,0:T(8,128)} %param.18) | copy-start | bytes 12292
  175.3 19.5 %all-to-all-start.2 = ((f32[8,128,256]{2,1,0:T(8,128)}), f32[8,128,256]{2,1,0:T(8,128)S(1)}, u32[]{:S(2)}, u32[]{:S(2)}) async-start(f32[8,128,256]{2,1,0:T(8,128)} %copy.41), calls=%async_computation.3 | async-start | bytes 2097152 | tf_op jit(solution)/shard_map/all_to_all | solution.py:85
  178.9 467.1 %all-reduce.2.cloned.1.call-start = ((), (), s32[]{:S(2)}) async-start(), calls=%async_computation.5 | async-start | bytes 524288 | tf_op jit(solution)/shard_map/psum | solution.py:100
  386.7 7.8 %copy-start.3 = (bf16[1,256,256]{2,1,0:T(8,128)(2,1)S(1)}, bf16[1,256,256]{2,1,0:T(8,128)(2,1)}, u32[]{:S(2)}) copy-start(bf16[1,256,256]{2,1,0:T(8,128)(2,1)} %param.10) | copy-start | bytes 393220
  386.7 261.1 %copy-start.1 = (bf16[1,1,64,128,128]{4,3,2,1,0:T(8,128)(2,1)S(1)}, bf16[1,1,64,128,128]{4,3,2,1,0:T(8,128)(2,1)}, u32[]{:S(2)}) copy-start(bf16[1,1,64,128,128]{4,3,2,1,0:T(8,128)(2,1)} %param.13) | copy-start | bytes 6291460
Sparse Core Ops, SparseCore 0:
  160.9 225.7 reduce-scatter.1
  396.5 249.4 all-reduce.1
